TPU v7x, 256 devices: a whole 4x4x8 slice. The times are simulated.
256 devices in a mesh: blk: 64 (over x, z, core), smp: 4 (over y).
Axes of the slice: x: 4, y: 4, z: 8, core: 2. Of those that a mesh axis runs over, the one named last changes fastest.
Arguments:
- encodings: bfloat16 [1024, 57344], P('smp', 'blk'), may hold values from -1 to 1
- hidden_pre: bfloat16 [1024, 8192], P('smp', 'blk'), may hold values from -6 to 6
- cotangent: bfloat16 [1024, 688128], P('smp', 'blk'), may hold values from -0.75 to 0.75
- out_weights: bfloat16 [10752, 128, 128], P('blk'), may hold values from -0.0390625 to 0.0390625
- out_contacts: int32 [5376, 2], P('blk'), may hold values from 0 to 63, all different within a row
- in_contacts: int32 [448, 4], P('blk'), may hold values from 0 to 63, all different within a row
Outputs:
- out_weight_grad: bfloat16 [10752, 128, 128], P(('blk', 'smp'))
- in_weight_grad: bfloat16 [1792, 128, 128], P(('blk', 'smp'))
Inputs may be any that keep to these rules, and one draw needn't show every extreme that they name: `out_contacts`: each row names 2 different hidden blocks, and every hidden block is named by some row. `in_contacts`: each row names 4 different hidden blocks, and every hidden block is named by some row.
All inputs are finite; a program needn't handle non-finite values.
Results may differ from a plain program's by a relative error of at most 0.0051.
Values may be sent and summed in bfloat16 or wider, within the bound.
No kernel may reach another device: no remote copies, remote signals or barrier semaphores. Data moves between devices by JAX's collectives and lax.ppermute only.
A program may use at most 128 MiB of HBM per device.

v0:
```python
import jax
import jax.numpy as jnp
from jax import lax
from jax.sharding import PartitionSpec as P


def silu_slope(values):
    sigma = jax.nn.sigmoid(values)
    return sigma * (1.0 + values * (1.0 - sigma))


def per_device(encodings, hidden_pre, cotangent, out_weights, out_contacts, in_contacts):
    sample_rows = cotangent.shape[0]
    block_size = out_weights.shape[1]
    out_local, per_out = out_contacts.shape
    in_local, per_in = in_contacts.shape
    pre_whole = lax.all_gather(hidden_pre, "blk", axis=1, tiled=True)
    hid_count = pre_whole.shape[1] // block_size
    pre_blocks = pre_whole.reshape(sample_rows, hid_count, block_size)
    activation = jax.nn.silu(pre_blocks.astype(jnp.float32)).astype(jnp.bfloat16)
    out_index = out_contacts.reshape(-1)
    in_index = in_contacts.reshape(-1)
    activ_taken = jnp.take(activation, out_index, axis=1).reshape(
        sample_rows, out_local, per_out, block_size
    )
    cot_blocks = cotangent.reshape(sample_rows, out_local, block_size)
    out_terms = jnp.einsum(
        "sokb,soc->okbc", activ_taken, cot_blocks, preferred_element_type=jnp.float32
    )
    out_terms = out_terms.reshape(out_local * per_out, block_size, block_size)
    out_grad = lax.psum_scatter(out_terms, "smp", scatter_dimension=0, tiled=True).astype(
        jnp.bfloat16
    )
    weight_view = out_weights.reshape(out_local, per_out, block_size, block_size)
    partial_terms = jnp.einsum(
        "soc,okbc->oksb", cot_blocks, weight_view, preferred_element_type=jnp.float32
    )
    partial_terms = partial_terms.reshape(out_local * per_out, sample_rows, block_size)
    hidden_terms = jax.ops.segment_sum(partial_terms, out_index, num_segments=hid_count)
    summed = lax.psum(hidden_terms, "blk")
    summed_taken = jnp.swapaxes(jnp.take(summed, in_index, axis=0), 0, 1)
    pre_taken = jnp.take(pre_blocks, in_index, axis=1).astype(jnp.float32)
    grad_taken = (summed_taken * silu_slope(pre_taken)).astype(jnp.bfloat16)
    grad_view = grad_taken.reshape(sample_rows, in_local, per_in, block_size)
    enc_blocks = encodings.reshape(sample_rows, in_local, block_size)
    in_terms = jnp.einsum(
        "sib,sikc->ikbc", enc_blocks, grad_view, preferred_element_type=jnp.float32
    )
    in_terms = in_terms.reshape(in_local * per_in, block_size, block_size)
    in_grad = lax.psum_scatter(in_terms, "smp", scatter_dimension=0, tiled=True).astype(
        jnp.bfloat16
    )
    return (out_grad, in_grad)


def solution(mesh):
    in_specs = (
        P("smp", "blk"),
        P("smp", "blk"),
        P("smp", "blk"),
        P("blk", None, None),
        P("blk", None),
        P("blk", None),
    )
    out_specs = (P(("blk", "smp"), None, None), P(("blk", "smp"), None, None))
    return jax.shard_map(
        per_device, mesh=mesh, in_specs=in_specs, out_specs=out_specs, check_vma=False
    )
```

profile of v0, /device:TPU:1, one launch (start us, length us, event | category | flops | bytes accessed | tf_op | source)
XLA Modules:
  0.0 569.7 jit_solution(5942079644765487091)
XLA Ops:
  7.2 8.3 %copy.36 = bf16[256,10752]{0,1:T(8,128)(2,1)} copy(bf16[256,10752]{1,0:T(8,128)(2,1)} %param.8) | data formatting | bytes 11010048 | tf_op args[2]
  15.5 14.6 %fusion.17 = f32[84,2,128,256]{3,2,1,0:T(8,128)} fusion(bf16[84,2,128,128]{3,2,1,0:T(8,128)(2,1)} %bitcast.57, bf16[256,84,128,1]{0,2,3,1:T(8,128)(2,1)} %bitcast.55), kind=kOutput, calls=%fused_computation.33 | convolution fusion | flops 1409286144 | bytes 33030144 | tf_op jit(solution)/shard_map/soc,okbc->oksb/dot_general | solution.py:35
  30.1 21.6 %copy.41 = f32[168,256,128]{2,1,0:T(8,128)} copy(f32[168,256,128]{1,2,0:T(8,128)} %bitcast.53) | data formatting | bytes 44040192 | tf_op jit(solution)/shard_map/reshape | solution.py:38
  52.0 4.4 broadcast_in_dim.36
  56.3 51.9 %scatter_fusion = f32[64,256,128]{2,1,0:T(8,128)} fusion(f32[64,256,128]{2,1,0:T(8,128)} %broadcast_in_dim.36, s32[168]{0:T(256)S(1)} %reshape.144, f32[168,256,128]{2,1,0:T(8,128)} %copy.41), kind=kCustom, calls=%fused_computation.3 | custom fusion | flops 5505024 | bytes 66060960 | tf_op jit(solution)/shard_map/scatter-add | solution.py:39
  108.3 0.8 copy-done.1
  109.0 0.7 copy.32
  110.1 0.2 copy.44
  110.4 205.8 %all-reduce.2.cloned.1.call-done = f32[64,256,128]{2,1,0:T(8,128)} async-done(((f32[64,256,128]{2,1,0:T(8,128)}), f32[64,256,128]{2,1,0:T(8,128)}) %all-reduce.2.cloned.1.call-update) | async-done | bytes 8388624 | tf_op jit(solution)/shard_map/psum | solution.py:40
  316.2 5.9 %gather_fusion.1 = f32[28,256,128]{2,1,0:T(8,128)} fusion(f32[64,256,128]{2,1,0:T(8,128)} %all-reduce.2.cloned.1.call-done, s32[1024]{0:T(1024)S(1)} %pad_clamp_fusion), kind=kCustom, calls=%fused_computation.1 | custom fusion | bytes 7340144 | tf_op jit(solution)/shard_map/jit(_take)/gather | solution.py:41
  322.2 77.4 %all-gather.2.cloned.1.call-done = bf16[256,8192]{0,1:T(8,128)(2,1)} async-done(((bf16[256,128]{0,1:T(8,128)(2,1)}), bf16[256,8192]{0,1:T(8,128)(2,1)}) %all-gather.2.cloned.1.call-update) | async-done | bytes 4194320 | tf_op jit(solution)/shard_map/all_gather | solution.py:17
  399.6 6.4 %copy.33 = bf16[256,64,128]{2,0,1:T(8,128)(2,1)} copy(bf16[256,64,128]{0,2,1:T(8,128)(2,1)} %bitcast.61) | data formatting | bytes 8388608 | tf_op jit(solution)/shard_map/reshape | solution.py:19
  405.9 3.1 gather_fusion.2
  409.0 3.8 fusion.14
  412.8 0.8 fusion.18
  413.6 1.7 copy.47
  415.3 0.2 reduce-scatter.3.cloned.1.call-start
  415.8 5.1 fusion.6
  420.9 10.0 %gather_fusion = bf16[168,256,128]{2,1,0:T(8,128)(2,1)} fusion(bf16[256,64,128]{2,0,1:T(8,128)(2,1)} %fusion.6, s32[1024]{0:T(1024)S(1)} %pad_clamp_fusion.1), kind=kCustom, calls=%fused_computation | custom fusion | bytes 22020768 | tf_op jit(solution)/shard_map/jit(_take)/gather | solution.py:23
  430.9 14.7 %copy.35 = bf16[256,84,2,128]{0,3,2,1:T(8,128)(2,1)} copy(bf16[256,84,2,128]{3,0,2,1:T(8,128)(2,1)} %bitcast.54) | data formatting | bytes 22020096 | tf_op jit(solution)/shard_map/jit(_take)/gather | solution.py:23
  445.6 13.0 %fusion = f32[84,2,128,128]{3,2,1,0:T(8,128)} fusion(bf16[256,84,128,1]{0,2,3,1:T(8,128)(2,1)} %bitcast.56, bf16[256,84,2,128]{0,3,2,1:T(8,128)(2,1)} %copy.35, pred[84,2]{1,0:T(8,128)(4,1)S(1)} %copy.31), kind=kOutput, calls=%fused_computation.4 | convolution fusion | flops 1414791168 | bytes 27525288 | tf_op jit(solution)/shard_map/sokb,soc->okbc/dot_general | solution.py:27
  458.7 1.7 convert_element_type.23
  460.4 99.7 %reduce-scatter.3.cloned.1.call-done = f32[42,128,128]{2,1,0:T(8,128)} async-done(((f32[168,128,128]{2,1,0:T(8,128)}), f32[42,128,128]{2,1,0:T(8,128)}) %reduce-scatter.3.cloned.1.call-update) | async-done | bytes 2752528 | tf_op jit(solution)/shard_map/reduce_scatter | solution.py:31
  560.1 3.1 convert_element_type.20
  (28 shorter events, 1.0 us)
Async XLA Ops:
  7.2 309.0 %all-reduce.2.cloned.1.call-start = ((), (), s32[]{:S(2)}) async-start(), calls=%async_computation.4 | async-start | bytes 16777216 | tf_op jit(solution)/shard_map/psum | solution.py:40
  30.1 21.7 %copy-start.3 = (s32[84,2]{0,1:T(2,128)S(1)}, s32[84,2]{0,1:T(2,128)}, u32[]{:S(2)}) copy-start(s32[84,2]{0,1:T(2,128)} %param.10) | copy-start | bytes 2020
  108.2 0.8 copy-start.1
  108.2 1.7 copy-start.2
  108.2 1.9 copy-start
  108.2 291.3 %all-gather.2.cloned.1.call-start = ((), (), s32[]{:S(2)}) async-start(), calls=%async_computation.2 | async-start | bytes 4259840 | tf_op jit(solution)/shard_map/all_gather | solution.py:17
  109.8 348.9 %reduce-scatter.5.cloned.1.call-start = ((), (), s32[]{:S(2)}) async-start(), calls=%async_computation.5 | async-start | bytes 2293760 | tf_op jit(solution)/shard_map/reduce_scatter | solution.py:50
  415.3 144.8 %reduce-scatter.3.cloned.1.call-start = ((), (), s32[]{:S(2)}) async-start(), calls=%async_computation.3 | async-start | bytes 13762560 | tf_op jit(solution)/shard_map/reduce_scatter | solution.py:31
Sparse Core Ops, SparseCore 0:
  108.3 207.8 all-reduce.1
  319.9 79.5 all-gather.1
  415.4 27.0 reduce-scatter.4
  458.8 101.2 reduce-scatter.2
where the time goes:
time: 571 us; the launch traced here: 570 us
  waiting for transfers between devices  383 us (67%)
  local copies, waits for them, and re-layouts  78.6 us (14%)
  other arithmetic  65.6 us (11%)
  matrix products  28.4 us (5%)
  between operations  13.9 us (2%)
    psum x1, waiting for transfers between devices, per_device(): summed = lax.psum(hidden_terms, 'blk')  206 us
    reduce_scatter x1, waiting for transfers between devices, per_device(): lax.psum_scatter(out_terms, 'smp', scatter_dimension=0, tiled=True)  99.7 us
    all_gather x1, waiting for transfers between devices, per_device(): pre_whole = lax.all_gather(hidden_pre, 'blk', axis=1, tiled=True)  77.4 us
    scatter-add x1, other arithmetic, per_device(): jax.ops.segment_sum(partial_terms, out_index, num_segments=hid_count)  51.9 us
    gather x2, local copies, waits for them, and re-layouts, per_device(): jnp.take(activation, out_index, axis=1)  24.7 us
    reshape x1, local copies, waits for them, and re-layouts, per_device(): partial_terms.reshape(out_local * per_out, sample_rows, block_size)  21.6 us
    dot_general x1, matrix products, per_device(): jnp.einsum('soc,okbc->oksb', cot_blocks, weight_view, preferred_element_t...  14.6 us
    dot_general x1, matrix products, per_device(): jnp.einsum('sokb,soc->okbc', activ_taken, cot_blocks, preferred_element_t...  13 us
  transfers between devices with their start and end apart: 4, of which 3 were waited for; matrix products, arithmetic and copies ran while one was open for 9% of the time, Pallas kernels for 0%

commit v1 on v0

--- a/solution.py
+++ b/solution.py
@@ -14,7 +14,9 @@
     block_size = out_weights.shape[1]
     out_local, per_out = out_contacts.shape
     in_local, per_in = in_contacts.shape
-    pre_whole = lax.all_gather(hidden_pre, "blk", axis=1, tiled=True)
+    pre_whole = jnp.concatenate(
+        lax.all_to_all(jnp.stack([hidden_pre] * lax.axis_size("blk")), "blk", 0, 0), axis=1
+    )
     hid_count = pre_whole.shape[1] // block_size
     pre_blocks = pre_whole.reshape(sample_rows, hid_count, block_size)
     activation = jax.nn.silu(pre_blocks.astype(jnp.float32)).astype(jnp.bfloat16)

time: 571 us -> 505 us (0.88)
  waiting for transfers between devices: 383 us -> 307 us
  starting transfers between devices: 0.34 us -> 13.5 us
    all_gather x1 -> x0, waiting for transfers between devices: 77.4 us -> none  [per_device(): pre_whole = lax.all_gather(hidden_pre, 'blk', axis=1, tiled=True)]
    all_to_all x0 -> x1, starting transfers between devices: none -> 13.2 us  [per_device(): lax.all_to_all(jnp.stack([hidden_pre] * lax.axis_size('blk')), 'blk', 0, 0)]
    reshape x1 -> x0, local copies, waits for them, and re-layouts: 6.37 us -> none  [per_device(): pre_blocks = pre_whole.reshape(sample_rows, hid_count, block_size)]
  transfers between devices with their start and end apart: 4 -> 4, of which waited for: 3 -> 2; matrix products, arithmetic and copies ran while one was open for 9% -> 30% of each run, Pallas kernels for 0% -> 0%
where the time goes in v1:
time: 505 us; the launch traced here: 503 us
  waiting for transfers between devices  307 us (61%)
  local copies, waits for them, and re-layouts  75.3 us (15%)
  other arithmetic  65.4 us (13%)
  matrix products  28.4 us (6%)
  between operations  13.8 us (3%)
  starting transfers between devices  13.5 us (3%)
    psum x1, waiting for transfers between devices, per_device(): summed = lax.psum(hidden_terms, 'blk')  204 us
    reduce_scatter x1, waiting for transfers between devices, per_device(): lax.psum_scatter(out_terms, 'smp', scatter_dimension=0, tiled=True)  103 us
    scatter-add x1, other arithmetic, per_device(): jax.ops.segment_sum(partial_terms, out_index, num_segments=hid_count)  51.7 us
    gather x2, local copies, waits for them, and re-layouts, per_device(): jnp.take(activation, out_index, axis=1)  24.7 us
    reshape x1, local copies, waits for them, and re-layouts, per_device(): partial_terms.reshape(out_local * per_out, sample_rows, block_size)  21.7 us
    dot_general x1, matrix products, per_device(): jnp.einsum('soc,okbc->oksb', cot_blocks, weight_view, preferred_element_t...  14.6 us
    all_to_all x1, starting transfers between devices, per_device(): lax.all_to_all(jnp.stack([hidden_pre] * lax.axis_size('blk')), 'blk', 0, 0)  13.2 us
    dot_general x1, matrix products, per_device(): jnp.einsum('sokb,soc->okbc', activ_taken, cot_blocks, preferred_element_t...  13 us
  transfers between devices with their start and end apart: 4, of which 2 were waited for; matrix products, arithmetic and copies ran while one was open for 30% of the time, Pallas kernels for 0%

profile of v1, /device:TPU:1, one launch (start us, length us, event | category | flops | bytes accessed | tf_op | source)
XLA Modules:
  0.0 503.3 jit_solution(11449421905022996017)
XLA Ops:
  7.2 3.8 stack.2
  11.0 13.2 %all-to-all-start = ((bf16[64,256,128]{2,1,0:T(8,128)(2,1)}), bf16[64,256,128]{2,1,0:T(8,128)(2,1)}, u32[]{:S(2)}, u32[]{:S(2)}) async-start(bf16[64,256,128]{2,1,0:T(8,128)(2,1)} %stack.2), calls=%async_computation | async-start | bytes 8388608 | tf_op jit(solution)/shard_map/all_to_all | solution.py:18
  24.2 8.3 %copy.18 = bf16[256,10752]{0,1:T(8,128)(2,1)} copy(bf16[256,10752]{1,0:T(8,128)(2,1)} %param.8) | data formatting | bytes 11010048 | tf_op args[2]
  32.5 14.6 %fusion.17 = f32[84,2,128,256]{3,2,1,0:T(8,128)} fusion(bf16[84,2,128,128]{3,2,1,0:T(8,128)(2,1)} %bitcast.58, bf16[256,84,128,1]{0,2,3,1:T(8,128)(2,1)} %bitcast.56), kind=kOutput, calls=%fused_computation.33 | convolution fusion | flops 1409286144 | bytes 33030144 | tf_op jit(solution)/shard_map/soc,okbc->oksb/dot_general | solution.py:37
  47.1 21.7 %copy.23 = f32[168,256,128]{2,1,0:T(8,128)} copy(f32[168,256,128]{1,2,0:T(8,128)} %bitcast.54) | data formatting | bytes 44040192 | tf_op jit(solution)/shard_map/reshape | solution.py:40
  69.0 4.4 broadcast_in_dim.36
  73.3 51.7 %scatter_fusion = f32[64,256,128]{2,1,0:T(8,128)} fusion(f32[64,256,128]{2,1,0:T(8,128)} %broadcast_in_dim.36, s32[168]{0:T(256)S(1)} %reshape.146, f32[168,256,128]{2,1,0:T(8,128)} %copy.23), kind=kCustom, calls=%fused_computation.3 | custom fusion | flops 5505024 | bytes 66060960 | tf_op jit(solution)/shard_map/scatter-add | solution.py:41
  125.1 0.6 copy-done.1
  126.1 0.2 copy.25
  126.4 203.9 %all-reduce.2.cloned.1.call-done = f32[64,256,128]{2,1,0:T(8,128)} async-done(((f32[64,256,128]{2,1,0:T(8,128)}), f32[64,256,128]{2,1,0:T(8,128)}) %all-reduce.2.cloned.1.call-update) | async-done | bytes 8388624 | tf_op jit(solution)/shard_map/psum | solution.py:42
  330.3 6.0 %gather_fusion.1 = f32[28,256,128]{2,1,0:T(8,128)} fusion(f32[64,256,128]{2,1,0:T(8,128)} %all-reduce.2.cloned.1.call-done, s32[1024]{0:T(1024)S(1)} %pad_clamp_fusion), kind=kCustom, calls=%fused_computation.1 | custom fusion | bytes 7340144 | tf_op jit(solution)/shard_map/jit(_take)/gather | solution.py:43
  336.3 3.1 gather_fusion.2
  339.4 3.8 fusion.14
  343.2 0.8 fusion.18
  343.9 1.7 copy.28
  345.7 0.2 reduce-scatter.3.cloned.1.call-start
  346.1 0.1 copy.15
  346.2 5.1 %fusion.6 = bf16[256,64,128]{2,0,1:T(8,128)(2,1)} fusion(bf16[64,256,128]{2,1,0:T(8,128)(2,1)} %all-to-all-done), kind=kLoop, calls=%fused_computation.12 | loop fusion | flops 12582912 | bytes 8388608 | tf_op jit(solution)/shard_map/convert_element_type | solution.py:22
  351.3 10.0 %gather_fusion = bf16[168,256,128]{2,1,0:T(8,128)(2,1)} fusion(bf16[256,64,128]{2,0,1:T(8,128)(2,1)} %fusion.6, s32[1024]{0:T(1024)S(1)} %pad_clamp_fusion.1), kind=kCustom, calls=%fused_computation | custom fusion | bytes 22020768 | tf_op jit(solution)/shard_map/jit(_take)/gather | solution.py:25
  361.3 14.7 %copy.17 = bf16[256,84,2,128]{0,3,2,1:T(8,128)(2,1)} copy(bf16[256,84,2,128]{3,0,2,1:T(8,128)(2,1)} %bitcast.55) | data formatting | bytes 22020096 | tf_op jit(solution)/shard_map/jit(_take)/gather | solution.py:25
  376.0 13.0 %fusion = f32[84,2,128,128]{3,2,1,0:T(8,128)} fusion(bf16[256,84,128,1]{0,2,3,1:T(8,128)(2,1)} %bitcast.57, bf16[256,84,2,128]{0,3,2,1:T(8,128)(2,1)} %copy.17, pred[84,2]{1,0:T(8,128)(4,1)S(1)} %copy.15), kind=kOutput, calls=%fused_computation.4 | convolution fusion | flops 1414791168 | bytes 27525288 | tf_op jit(solution)/shard_map/sokb,soc->okbc/dot_general | solution.py:29
  389.0 1.7 convert_element_type.23
  390.8 102.9 %reduce-scatter.3.cloned.1.call-done = f32[42,128,128]{2,1,0:T(8,128)} async-done(((f32[168,128,128]{2,1,0:T(8,128)}), f32[42,128,128]{2,1,0:T(8,128)}) %reduce-scatter.3.cloned.1.call-update) | async-done | bytes 2752528 | tf_op jit(solution)/shard_map/reduce_scatter | solution.py:33
  493.7 3.1 convert_element_type.20
  (24 shorter events, 0.9 us)
Async XLA Ops:
  11.0 325.3 %all-to-all-start = ((bf16[64,256,128]{2,1,0:T(8,128)(2,1)}), bf16[64,256,128]{2,1,0:T(8,128)(2,1)}, u32[]{:S(2)}, u32[]{:S(2)}) async-start(bf16[64,256,128]{2,1,0:T(8,128)(2,1)} %stack.2), calls=%async_computation | async-start | bytes 8388608 | tf_op jit(solution)/shard_map/all_to_all | solution.py:18
  24.1 306.1 %all-reduce.2.cloned.1.call-start = ((), (), s32[]{:S(2)}) async-start(), calls=%async_computation.4 | async-start | bytes 16777216 | tf_op jit(solution)/shard_map/psum | solution.py:42
  47.1 21.7 %copy-start.2 = (s32[84,2]{0,1:T(2,128)S(1)}, s32[84,2]{0,1:T(2,128)}, u32[]{:S(2)}) copy-start(s32[84,2]{0,1:T(2,128)} %param.10) | copy-start | bytes 2020
  125.1 0.7 copy-start.1
  125.1 1.0 copy-start
  125.1 263.9 %reduce-scatter.5.cloned.1.call-start = ((), (), s32[]{:S(2)}) async-start(), calls=%async_computation.5 | async-start | bytes 2293760 | tf_op jit(solution)/shard_map/reduce_scatter | solution.py:52
  345.7 148.0 %reduce-scatter.3.cloned.1.call-start = ((), (), s32[]{:S(2)}) async-start(), calls=%async_computation.3 | async-start | bytes 13762560 | tf_op jit(solution)/shard_map/reduce_scatter | solution.py:33
Sparse Core Ops, SparseCore 0:
  125.2 205.0 all-reduce.1
  345.8 30.3 reduce-scatter.4
  389.1 104.5 reduce-scatter.2
